TPU v7x, 512 devices: a whole 4x4x16 slice. The times are simulated.
512 devices in a mesh: outer: 32 (over x_lo, z), dev: 16 (over x_hi, y, core).
Axes of the slice: x: 4 (x_hi: 2, x_lo: 2; x = x_hi * 2 + x_lo), y: 4, z: 16, core: 2. Of those that a mesh axis runs over, the one named last changes fastest.
Arguments:
- grads: float32 [32, 16, 1048576], P('outer', 'dev'), may hold values from -6 to 6
- residual: float32 [32, 1048576], P('outer', 'dev'), may hold values from -24 to 24
- sign_bits: int32 [1024], replicated, may hold values from 0 to 1
- kept_index: int32 [1024], replicated, may hold values from 0 to 7
Outputs:
- synced: float32 [1048576], replicated
- new_residual: float32 [32, 1048576], P('outer', 'dev')
All inputs are finite; a program needn't handle non-finite values.
Results may differ from a plain program's by a relative error of at most 0.000073.
Values sent between devices are 32-bit elements; how exact they have to be, the bound alone decides.
A program may use at most 64 MiB of HBM per device.

v0:
```python
import math

import jax
import jax.numpy as jnp
import numpy as np
from jax import lax
from jax.sharding import PartitionSpec as P

HAD = 1024
KEEP = 128


def hadamard_table():
    index = np.arange(HAD)
    common = index[:, None] & index[None, :]
    parity = np.zeros((HAD, HAD), np.int64)
    for bit in range(HAD.bit_length()):
        parity = parity ^ common >> bit & 1
    return jnp.asarray(((1 - 2 * parity) / math.sqrt(HAD)).astype(np.float32))


def select_runs(values, picks):
    onehot = (picks[:, None] == jnp.arange(8, dtype=jnp.int32)[None, :]).astype(jnp.float32)
    return jnp.sum(values.reshape(-1, 8, KEEP) * onehot[:, :, None], axis=1)


def decode_runs(sketch, picks, sign_vec, table):
    onehot = (picks[:, None] == jnp.arange(8, dtype=jnp.int32)[None, :]).astype(jnp.float32)
    placed = (sketch[:, None, :] * onehot[:, :, None]).reshape(-1, HAD)
    return (jnp.dot(placed, table, precision=lax.Precision.HIGHEST) * sign_vec[None, :]).reshape(-1)


def shards(grads, residual, sign_bits, kept_index):
    table = hadamard_table()
    sign_vec = (1 - 2 * sign_bits).astype(jnp.float32)
    shard = lax.psum_scatter(grads.reshape(-1), "dev", scatter_dimension=0, tiled=True)
    corrected = shard + residual.reshape(-1)
    own_blocks = corrected.shape[0] // HAD
    first = lax.axis_index("dev") * own_blocks
    own_picks = lax.dynamic_slice_in_dim(kept_index, first, own_blocks, 0)
    blocks = corrected.reshape(-1, HAD) * sign_vec[None, :]
    spread = jnp.dot(blocks, table, precision=lax.Precision.HIGHEST)
    kept = select_runs(spread, own_picks)
    new_residual = corrected - decode_runs(kept, own_picks, sign_vec, table)
    pods = lax.axis_size("outer")
    total = lax.psum(kept, "outer")
    local_part = decode_runs(total, own_picks, sign_vec, table) / pods
    synced = lax.all_gather(local_part, "dev", axis=0, tiled=True)
    return (synced, new_residual.reshape(1, -1))


def solution(mesh):
    in_specs = (P("outer", "dev", None), P("outer", "dev"), P(), P())
    out_specs = (P(), P("outer", "dev"))
    return jax.shard_map(shards, mesh=mesh, in_specs=in_specs, out_specs=out_specs, check_vma=False)
```

profile of v0, /device:TPU:1, one launch (start us, length us, event | category | flops | bytes accessed | tf_op | source)
XLA Modules:
  0.0 388.5 jit_solution(5656275138445727135)
XLA Ops:
  7.2 0.0 copy-start.1
  7.2 0.0 copy-start
  7.2 0.0 all-reduce.3.cloned.1.call-start
  7.2 0.7 all-reduce.3.cloned.1.call-update
  7.9 0.0 all-gather.2.cloned.1.call-start
  8.0 0.0 copy-done.1
  8.1 0.8 dynamic_slice.3
  8.8 1.3 dynamic-slice
  10.8 170.9 %all-reduce.3.cloned.1.call-done = f32[1048576]{0:T(1024)} async-done(((f32[1048576]{0:T(1024)}), f32[1048576]{0:T(1024)}) %all-reduce.3.cloned.1.call-update) | async-done | bytes 4194320
  181.6 0.0 copy-done
  181.7 1.0 fusion.5
  182.7 6.3 %fusion.3 = f32[64,128]{1,0:T(8,128)S(1)} fusion(f32[64,1024,1]{1,0,2:T(8,128)S(1)} %reshape.61, f32[8,128,1024]{2,1,0:T(8,128)} %constant.25, f32[64,8]{0,1:T(8,128)S(1)} %fusion.6), kind=kOutput, calls=%fused_computation.6 | convolution fusion | flops 805429248 | bytes 4491264 | tf_op jit(solution)/shard_map/dot_general | solution.py:42
  189.0 94.6 %psum.7 = f32[64,128]{1,0:T(8,128)S(1)} all-reduce(f32[64,128]{1,0:T(8,128)S(1)} %fusion.3), channel_id=1, replica_groups=mesh['outer'=32,'dev'=16] {'outer'}, use_global_device_ids=true, to_apply=%region_2.0 | all-reduce | flops 8192 | bytes 65536 | tf_op jit(solution)/shard_map/psum | solution.py:46
  283.6 0.1 multiply_bitcast_fusion
  283.7 4.8 %fusion.2 = f32[8,8,8,128]{3,2,1,0:T(8,128)S(1)} fusion(f32[1024,1024]{1,0:T(8,128)} %constant.21.clone, f32[8,8,8,128]{3,2,1,0:T(8,128)S(1)} %get-tuple-element.3, f32[1024]{0:T(1024)S(1)} %subtract_convert_fusion), kind=kOutput, calls=%fused_computation.4 | convolution fusion | flops 805437440 | bytes 4722688 | tf_op jit(solution)/shard_map/dot_general | solution.py:30
  288.5 0.8 copy.14
  289.3 0.0 all-gather.2.cloned.1.call-update
  289.3 4.8 %fusion = f32[8,8,8,128]{3,2,1,0:T(8,128)S(1)} fusion(f32[1024,1024]{1,0:T(8,128)} %constant.21.clone, f32[8,8,8,128]{3,2,1,0:T(8,128)S(1)} %get-tuple-element.2, f32[1024]{0:T(1024)S(1)} %subtract_convert_fusion), kind=kOutput, calls=%fused_computation.1 | convolution fusion | flops 805371904 | bytes 4722688 | tf_op jit(solution)/shard_map/dot_general | solution.py:30
  294.2 1.7 fusion.4
  295.9 81.3 %all-gather.2.cloned.1.call-done = f32[1048576]{0:T(1024)} async-done(((f32[65536]{0:T(1024)}), f32[1048576]{0:T(1024)}) %all-gather.2.cloned.1.call-update) | async-done | bytes 4194320 | tf_op jit(solution)/shard_map/all_gather | solution.py:48
  377.2 4.5 %copy.23 = f32[1048576]{0:T(1024)} copy(f32[1048576]{0:T(1024)} %all-gather.2.cloned.1.call-done) | data formatting | bytes 8388608
  (6 shorter events, 0.2 us)
Async XLA Ops:
  7.2 0.8 copy-start.1
  7.2 174.5 %copy-start = (f32[1,65536]{1,0:T(1,128)S(1)}, f32[1,65536]{1,0:T(1,128)}, u32[]{:S(2)}) copy-start(f32[1,65536]{1,0:T(1,128)} %param.6) | copy-start | bytes 786436
  7.2 174.5 %all-reduce.3.cloned.1.call-start = ((), (), s32[]{:S(2)}) async-start(), calls=%async_computation.1 | async-start | bytes 8388608
  7.9 369.3 %all-gather.2.cloned.1.call-start = ((), (), s32[]{:S(2)}) async-start(), calls=%async_computation | async-start | bytes 4456448 | tf_op jit(solution)/shard_map/all_gather | solution.py:48
Sparse Core Ops, SparseCore 0:
  11.0 170.6 all-reduce.2
  289.4 87.7 all-gather.1
where the time goes:
time: 389 us
  waiting for transfers between devices  253 us (65%)
  blocking collectives  94.6 us (24%)
  matrix products  15.9 us (4%)
  between operations  14.8 us (4%)
  local copies, waits for them, and re-layouts  7.42 us (2%)
    unnamed x3, waiting for transfers between devices  172 us
    psum x1, blocking collectives, shards(): total = lax.psum(kept, 'outer')  94.6 us
    all_gather x1, waiting for transfers between devices, shards(): synced = lax.all_gather(local_part, 'dev', axis=0, tiled=True)  81.3 us
    dot_general x2, matrix products, decode_runs(): jnp.dot(placed, table, precision=lax.Precision.HIGHEST) * sign_vec[None, :]  9.67 us
  transfers between devices with their start and end apart: 2, of which 2 were waited for; matrix products, arithmetic and copies ran while one was open for 2% of the time, Pallas kernels for 0%

commit v1 on v0

v1 whole, which is shorter than its diff:
```python
import jax
import jax.numpy as jnp
from jax import lax
from jax.experimental import pallas as pl
from jax.experimental.pallas import tpu as pltpu
from jax.sharding import PartitionSpec as P

MESH = pl.DeviceIdType.MESH
F32 = jnp.float32
LANES = 128
SHARD = 512
CHUNK = 16
FIRST = 208


def place():
    o, d = lax.axis_index("outer"), lax.axis_index("dev")
    x = (d // 8) * 2 + o // 16
    return x, (d // 2) % 4, (o % 16) // 2, o % 2, d % 2


def device(x, y, zg, zp, c):
    return ((x % 2) * 16 + zg * 2 + zp, (x // 2) * 8 + y * 2 + c)


def rows(start, size, multiple):
    return pl.ds(pl.multiple_of(start, multiple), size)


def spread_index(row):
    return jnp.transpose(jnp.broadcast_to(row.astype(F32), (LANES, LANES))).astype(jnp.int32)


def flips(k):
    return [(1 - 2 * ((k >> bit) & 1)).astype(F32) for bit in range(3)]


def fold(t, s):
    u = [t[2 * i] + s[0] * t[2 * i + 1] for i in range(4)]
    v = [u[0] + s[1] * u[1], u[2] + s[1] * u[3]]
    return v[0] + s[2] * v[1]


def unfold(w, s):
    a = [w, s[2] * w]
    b = [a[0], s[1] * a[0], a[1], s[1] * a[1]]
    return [e for p in b for e in (p, s[0] * p)]


def comm_kernel(
    g, res_in, bits_in, picks_in, tot, newres,
    res, bits, picks, gbuf, cin, kb, kept_o, kept_m, kcin, rsin, zin, y1in, x1in, x2in, y2in,
    isem, lsem, ksend, krecv, csend, crecv, rsend, rrecv, zsend, zrecv, asend, arecv,
    tsend, trecv, y1s, y1r, x1s, x1r, x2s, x2r, y2s, y2r,
):
    x, y, zg, zp, c = place()
    xh, xl = x // 2, x % 2
    oc = 1 - c
    mine = xh * 4 + y
    other_core = device(x, y, zg, zp, oc)

    def near(i):
        dx, dy, dp = i // 8, (i // 2) % 4, i % 2
        return (x + dx) % 4, (y + dy) % 4, (zp + dp) % 2

    def copy(src, dst, ssem, rsem, dev):
        cp = pltpu.make_async_remote_copy(
            src_ref=src, dst_ref=dst, send_sem=ssem, recv_sem=rsem, device_id=dev, device_id_type=MESH
        )
        cp.start()

    def wait(ref, sem):
        pltpu.make_async_copy(ref, ref, sem).wait()

    bar = pltpu.get_barrier_semaphore()

    def greet(dev):
        pl.semaphore_signal(bar, inc=1, device_id=dev, device_id_type=MESH)

    def greet_far(i, _):
        greet(device(x, y, (zg + i) % 8, zp, c))
        return 0

    def greet_near(i, _):
        px, py, pp = near(i)
        greet(device(px, py, zg, pp, c))
        return 0

    small = [(picks_in, picks), (bits_in, bits), (res_in, res)]
    small = [pltpu.make_async_copy(a, b, isem.at[i]) for i, (a, b) in enumerate(small)]
    small[0].start()
    small[1].start()
    lax.fori_loop(1, 8, greet_far, 0)
    lax.fori_loop(1, 32, greet_near, 0)
    greet(other_core)

    def load(s, core):
        r = rows((s * 2 + core) * SHARD, SHARD, SHARD)
        return pltpu.make_async_copy(g.at[r], gbuf.at[r], lsem.at[s * 2 + core])

    for s in range(8):
        load(s, oc).start()
    for s in range(8):
        load(s, c).start()

    small[2].start()

    small[0].wait()
    small[1].wait()
    for t in range(8):
        kb[t * LANES : (t + 1) * LANES, :] = spread_index(picks[t : t + 1, :])
    sgn = (1 - 2 * bits[...]).astype(F32)
    sg = [sgn[j : j + 1, :] for j in range(8)]

    def fold_rows(ref, row0, block0):
        t = [ref[pl.ds(row0 + j, 8, stride=8), :] * sg[j] for j in range(8)]
        return fold(t, flips(kb[rows(block0, 8, 8), :]))

    def fold_shard(s, core, dst):
        def body(i, _):
            row0 = pl.multiple_of((s * 2 + core) * SHARD + i * 64, 64)
            dst[rows(s * 64 + i * 8, 8, 8), :] = fold_rows(gbuf, row0, (s * 2 + core) * 64 + i * 8)
            return 0

        lax.fori_loop(0, 8, body, 0, unroll=4)

    for s in range(8):
        load(s, oc).wait()
        fold_shard(s, oc, kept_o)

    pl.semaphore_wait(bar, 39)

    copy(kept_o, kcin, ksend, krecv, other_core)
    for s in range(8):
        r = rows((s * 2 + oc) * SHARD, SHARD, SHARD)
        copy(gbuf.at[r], cin.at[s * SHARD : (s + 1) * SHARD], csend.at[s], crecv.at[s], other_core)

    for s in range(8):
        load(s, c).wait()
        fold_shard(s, c, kept_m)

    small[2].wait()

    def add_residual(i, _):
        r = rows(mine * 64 + i * 8, 8, 8)
        kept_m[r, :] += fold_rows(res, i * 64, (mine * 2 + c) * 64 + i * 8)
        return 0

    lax.fori_loop(0, 8, add_residual, 0)

    wait(kcin, krecv)

    def add_kept(i, _):
        r = rows(i * 64, 64, 64)
        kept_m[r, :] += kcin[r, :]
        return 0

    lax.fori_loop(0, 8, add_kept, 0)

    def chunk_row(px, py, pp):
        return ((px // 2) * 4 + py) * 64 + ((px % 2) * 2 + pp) * CHUNK

    def send_chunk(i, _):
        px, py, pp = near(i)
        copy(
            kept_m.at[rows(chunk_row(px, py, pp), CHUNK, CHUNK)],
            rsin.at[rows(i * CHUNK, CHUNK, CHUNK)],
            rsend, rrecv, device(px, py, zg, pp, c),
        )
        return 0

    lax.fori_loop(1, 32, send_chunk, 0)

    def own_row(s):
        return (s * 2 + c) * SHARD

    def add_core(s):
        wait(cin.at[s * SHARD : (s + 1) * SHARD], crecv.at[s])

        def body(i, _):
            r = rows(own_row(s) + i * 64, 64, 64)
            gbuf[r, :] += cin[rows(s * SHARD + i * 64, 64, 64), :]
            return 0

        lax.fori_loop(0, 8, body, 0)

    for s in range(8):
        add_core(s)

    rest = SHARD - FIRST
    across = device(x + 2 - 4 * xh, y, zg, zp, c)

    def along(dy):
        return device(x, (y + dy) % 4, zg, zp, c)

    for dy in (2, 1, 3):
        py = (y + dy) % 4
        for h in range(2):
            copy(
                gbuf.at[rows(own_row(h * 4 + py), FIRST, 16)],
                y1in.at[pl.ds(((dy - 1) * 2 + h) * FIRST, FIRST)],
                y1s.at[dy - 1], y1r.at[dy - 1], along(dy),
            )
    for py in range(4):
        copy(
            gbuf.at[rows(own_row((1 - xh) * 4 + py) + FIRST, rest, 16)],
            x1in.at[pl.ds(py * rest, rest)],
            x1s, x1r, across,
        )

    wait(rsin.at[CHUNK:], rrecv)
    my_row = chunk_row(x, y, zp)
    total = kept_m[rows(my_row, CHUNK, CHUNK), :]
    for i in range(1, 32):
        total = total + rsin[i * CHUNK : (i + 1) * CHUNK, :]
    zin[rows(zg * CHUNK, CHUNK, CHUNK), :] = total

    def send_far(i, _):
        r = rows(zg * CHUNK, CHUNK, CHUNK)
        copy(zin.at[r], zin.at[r], zsend, zrecv, device(x, y, (zg + i) % 8, zp, c))
        return 0

    lax.fori_loop(1, 8, send_far, 0)

    wait(x1in, x1r)
    for py in range(4):
        def body(i, _, py=py):
            r = rows(own_row(xh * 4 + py) + FIRST + i * 16, 16, 16)
            gbuf[r, :] += x1in[rows(py * rest + i * 16, 16, 16), :]
            return 0

        lax.fori_loop(0, rest // 16, body, 0, unroll=4)
    for dy in (2, 1, 3):
        copy(
            gbuf.at[rows(own_row(xh * 4 + (y + dy) % 4) + FIRST, rest, 16)],
            y2in.at[pl.ds((dy - 1) * rest, rest)],
            y2s.at[dy - 1], y2r.at[dy - 1], along(dy),
        )
    for dy in (1, 2, 3):
        wait(y1in.at[pl.ds((dy - 1) * 2 * FIRST, 2 * FIRST)], y1r.at[dy - 1])
    for h in range(2):
        def body(i, _, h=h):
            r = rows(own_row(h * 4 + y) + i * 16, 16, 16)
            a = [y1in[rows((2 * k + h) * FIRST + i * 16, 16, 16), :] for k in range(3)]
            gbuf[r, :] += a[0] + a[1] + a[2]
            return 0

        lax.fori_loop(0, FIRST // 16, body, 0, unroll=2)
    copy(gbuf.at[rows(own_row((1 - xh) * 4 + y), FIRST, 16)], x2in, x2s, x2r, across)

    wait(zin.at[0 : 7 * CHUNK], zrecv)
    z = [zin[i * CHUNK : (i + 1) * CHUNK, :] for i in range(8)]
    chunk = rows(c * 512 + my_row, CHUNK, CHUNK)
    tot[chunk, :] = ((z[0] + z[1]) + (z[2] + z[3])) + ((z[4] + z[5]) + (z[6] + z[7]))

    def send_total(i, _):
        px, py, pp = near(i)
        copy(tot.at[chunk], tot.at[chunk], asend, arecv, device(px, py, zg, pp, c))
        return 0

    lax.fori_loop(1, 32, send_total, 0)

    wait(x2in, x2r)
    for dy in (1, 2, 3):
        wait(y2in.at[pl.ds((dy - 1) * rest, rest)], y2r.at[dy - 1])
    base = own_row(mine)

    def add_x(i, _):
        r = rows(base + i * 16, 16, 16)
        gbuf[r, :] += x2in[rows(i * 16, 16, 16), :] + res[rows(i * 16, 16, 16), :]
        return 0

    lax.fori_loop(0, FIRST // 16, add_x, 0)

    def add_y(i, _):
        r = rows(base + FIRST + i * 16, 16, 16)
        a = [y2in[rows(k * rest + i * 16, 16, 16), :] for k in range(3)]
        gbuf[r, :] += (a[0] + a[1]) + (a[2] + res[rows(FIRST + i * 16, 16, 16), :])
        return 0

    lax.fori_loop(0, rest // 16, add_y, 0)

    def subtract(i, _):
        row0 = pl.multiple_of(base + i * 64, 64)
        t = [gbuf[pl.ds(row0 + j, 8, stride=8), :] for j in range(8)]
        s = flips(kb[rows((mine * 2 + c) * 64 + i * 8, 8, 8), :])
        w = fold([t[j] * sg[j] for j in range(8)], s) * 0.125
        for j, e in enumerate(unfold(w, s)):
            newres[pl.ds(pl.multiple_of(i * 64, 64) + j, 8, stride=8), :] = t[j] - e * sg[j]
        return 0

    lax.fori_loop(0, 8, subtract, 0)

    wait(tot.at[0 : 31 * CHUNK], arecv)
    half = rows(c * 512, 512, 512)
    copy(tot.at[half], tot.at[half], tsend, trecv, other_core)
    wait(tot.at[half], trecv)

    wait(kept_o, ksend)
    for s in range(8):
        wait(cin.at[s * SHARD : (s + 1) * SHARD], csend.at[s])
    wait(rsin.at[CHUNK:], rsend)
    wait(zin.at[0 : 7 * CHUNK], zsend)
    wait(tot.at[0 : 31 * CHUNK], asend)
    wait(tot.at[half], tsend)
    for dy in (1, 2, 3):
        wait(y1in.at[pl.ds((dy - 1) * 2 * FIRST, 2 * FIRST)], y1s.at[dy - 1])
        wait(y2in.at[pl.ds((dy - 1) * rest, rest)], y2s.at[dy - 1])
    wait(x1in, x1s)
    wait(x2in, x2s)


def decode_kernel(tot, bits, picks, res_in, synced, res_out):
    step = pl.program_id(0)
    res_out[...] = res_in[...]
    sgn = (1 - 2 * bits[...]).astype(F32)
    k = spread_index(picks[pl.ds(step, 1), :])
    for core in range(2):
        for i in range(8):
            at = core * 64 + i * 8
            w = tot[core, i * 8 : (i + 1) * 8, :] * (1.0 / 256.0)
            for j, e in enumerate(unfold(w, flips(k[at : at + 8, :]))):
                synced[pl.ds(at * 8 + j, 8, stride=8), :] = e * sgn[j : j + 1, :]


def shards(grads, residual, sign_bits, kept_index):
    g = grads.reshape(8192, LANES)
    res = residual.reshape(SHARD, LANES)
    bits = sign_bits.reshape(8, LANES)
    picks = kept_index.reshape(8, LANES)
    rest = SHARD - FIRST
    vmem = pl.BlockSpec(memory_space=pltpu.VMEM)
    dma = pltpu.SemaphoreType.DMA

    def buf(n, kind=F32):
        return pltpu.VMEM((n, LANES), kind)

    tot, newres = pl.pallas_call(
        comm_kernel,
        name="sum_pods",
        out_shape=(jax.ShapeDtypeStruct((1024, LANES), F32), jax.ShapeDtypeStruct((SHARD, LANES), F32)),
        in_specs=[pl.BlockSpec(memory_space=pltpu.HBM)] * 4,
        out_specs=(vmem, vmem),
        scratch_shapes=[
            buf(512), buf(8, jnp.int32), buf(8, jnp.int32), buf(8192), buf(4096), buf(1024, jnp.int32), buf(512), buf(512), buf(512),
            buf(32 * CHUNK), buf(8 * CHUNK), buf(6 * FIRST), buf(4 * rest), buf(FIRST), buf(3 * rest),
            dma((3,)), dma((16,)), dma, dma, dma((8,)), dma((8,)), dma, dma, dma, dma, dma, dma,
            dma, dma, dma((3,)), dma((3,)), dma, dma, dma, dma, dma((3,)), dma((3,)),
        ],
        compiler_params=pltpu.CompilerParams(
            collective_id=0, has_side_effects=True, vmem_limit_bytes=60 << 20
        ),
    )(g, res, bits, picks)

    whole = pl.BlockSpec((8, LANES), lambda i: (0, 0))
    synced, new_residual = pl.pallas_call(
        decode_kernel,
        name="decode",
        grid=(8,),
        out_shape=(jax.ShapeDtypeStruct((8192, LANES), F32), jax.ShapeDtypeStruct((SHARD, LANES), F32)),
        in_specs=[
            pl.BlockSpec((2, 64, LANES), lambda i: (0, i, 0)),
            whole,
            whole,
            pl.BlockSpec((64, LANES), lambda i: (i, 0)),
        ],
        out_specs=(
            pl.BlockSpec((1024, LANES), lambda i: (i, 0)),
            pl.BlockSpec((64, LANES), lambda i: (i, 0)),
        ),
    )(tot.reshape(2, 512, LANES), bits, picks, newres)
    return synced.reshape(-1), new_residual.reshape(1, -1)


def solution(mesh):
    in_specs = (P("outer", "dev", None), P("outer", "dev"), P(), P())
    out_specs = (P(), P("outer", "dev"))
    return jax.shard_map(shards, mesh=mesh, in_specs=in_specs, out_specs=out_specs, check_vma=False)
```

time: 389 us -> 61.3 us (0.16)
  waiting for transfers between devices: 253 us -> 0 us
  blocking collectives: 94.6 us -> 0 us
  Pallas kernels: 0 us -> 60.2 us
  matrix products: 15.9 us -> 0 us
  between operations: 14.8 us -> 0.64 us
  local copies, waits for them, and re-layouts: 7.42 us -> 0 us
    unnamed x3 -> x0, waiting for transfers between devices: 172 us -> none
    psum x1 -> x0, blocking collectives: 94.6 us -> none  [shards(): total = lax.psum(kept, 'outer')]
    all_gather x1 -> x0, waiting for transfers between devices: 81.3 us -> none  [shards(): synced = lax.all_gather(local_part, 'dev', axis=0, tiled=True)]
    pallas_call x0 -> x2, Pallas kernels: none -> 60.2 us  [the longest x1 54.2 us: shards(): pl.pallas_call(comm_kernel, name='sum_pods', out_shape=(jax.ShapeDtypeStr...]
    dot_general x3 -> x0, matrix products: 15.9 us -> none  [the longest x2 9.67 us: decode_runs(): jnp.dot(placed, table, precision=lax.Precision.HIGHEST) * sign_vec[None, :]]
    unnamed x10 -> x0, local copies, waits for them, and re-layouts: 6.61 us -> none
  transfers between devices with their start and end apart: 2 -> 0, of which waited for: 2 -> 0; matrix products, arithmetic and copies ran while one was open for 2% -> 0% of each run, Pallas kernels for 0% -> 0%
where the time goes in v1:
time: 61.3 us; the launch traced here: 60.8 us
  Pallas kernels  60.2 us (98%)
  between operations  0.64 us (1%)
    pallas_call x1, Pallas kernels, shards(): pl.pallas_call(comm_kernel, name='sum_pods', out_shape=(jax.ShapeDtypeStr...  54.2 us
    pallas_call x1, Pallas kernels, shards(): pl.pallas_call(decode_kernel, name='decode', grid=(8,), out_shape=(jax.Sh...  5.98 us

profile of v1, /device:TPU:1, one launch (start us, length us, event | category | flops | bytes accessed | tf_op | source)
XLA Modules:
  0.0 60.8 jit_solution(9660227422398564758)
XLA Ops:
  0.6 54.2 %sum_pods.1 = (f32[1024,128]{1,0:T(8,128)}, f32[512,128]{1,0:T(8,128)}) custom-call(f32[8192,128]{1,0:T(8,128)} %bitcast.7, f32[512,128]{1,0:T(8,128)} %bitcast.9, s32[8,128]{1,0:T(8,128)} %bitcast.10, s32[8,128]{1,0:T(8,128)} %bitcast.12), custom_call_target="tpu_custom_call" | custom-call | tf_op jit(solution)/shard_map/sum_pods/pallas_call | solution.py:338
  54.8 6.0 %decode.1 = (f32[8192,128]{1,0:T(8,128)}, f32[512,128]{1,0:T(8,128)}) custom-call(f32[2,512,128]{2,1,0:T(8,128)} %bitcast.8, s32[8,128]{1,0:T(8,128)} %bitcast.11, s32[8,128]{1,0:T(8,128)} %bitcast.13, f32[512,128]{1,0:T(8,128)} %get-tuple-element.7.res_in), custom_call_target="tpu_custom_call" | custom-call | tf_op jit(solution)/shard_map/decode/pallas_call | solution.py:356

commit v2 on v0

v2 whole, which is shorter than its diff:
```python
import jax
import jax.numpy as jnp
from jax import lax
from jax.experimental import pallas as pl
from jax.experimental.pallas import tpu as pltpu
from jax.sharding import PartitionSpec as P

MESH = pl.DeviceIdType.MESH
F32 = jnp.float32
LANES = 128
SHARD = 512
CHUNK = 16
X_FIRST = (1, 3, 5, 7)
Y_FIRST = (2, 4, 6)
NEAR = sorted(
    ((dx, dy, dp) for dx in range(4) for dy in range(4) for dp in range(2) if dx + dy + dp),
    key=lambda d: -(min(d[0], 4 - d[0]) + min(d[1], 4 - d[1]) + d[2]),
)
FAR = (4, 3, 5, 2, 6, 1, 7)


def rows(start, size, multiple):
    return pl.ds(pl.multiple_of(start, multiple), size)


def spread_index(row):
    return jnp.transpose(jnp.broadcast_to(row.astype(F32), (LANES, LANES))).astype(jnp.int32)


def row_signs(k):
    s = [(1 - 2 * ((k >> bit) & 1)).astype(F32) for bit in range(3)]
    s01 = s[0] * s[1]
    return [None, s[0], s[1], s01, s[2], s[0] * s[2], s[1] * s[2], s01 * s[2]]


def times(a, b):
    return a if b is None else a * b


def transform(t):
    for step in (1, 2, 4):
        out = [None] * 8
        for i in range(8):
            if i & step == 0:
                p, q = t[i], t[i | step]
                out[i], out[i | step] = (q, -q) if p is None else (p + q, p - q)
        t = out
    return t


def comm_kernel(
    g, res_in, bits_in, picks_in, tot, newres,
    res, bits, picks, gbuf, coef, cin, kb, rcoef, rsin, zin, y1in, x1in, x2in, y2in,
    isem, lsem, csend, crecv, rsend, rrecv, zsend, zrecv, asend, arecv,
    tsend, trecv, y1s, y1r, x1s, x1r, x2s, x2r, y2s, y2r,
):
    o, d = lax.axis_index("outer"), lax.axis_index("dev")
    xh, xl, zg, zp = d // 8, o // 16, (o % 16) // 2, o % 2
    y, c = (d // 2) % 4, d % 2
    oc = 1 - c
    mine = xh * 4 + y

    ys = [y] + [(y + i) % 4 for i in (1, 2, 3)]
    xs = [(xh, xl)] + [((xh + (xl + i) // 2) % 2, (xl + i) % 2) for i in (1, 2, 3)]
    zgs = [zg] + [(zg + i) % 8 for i in range(1, 8)]
    zps = [zp, 1 - zp]

    def device(dx=0, dy=0, dp=0, far=0, core=None):
        h, l = xs[dx]
        return (l * 16 + zgs[far] * 2 + zps[dp], h * 8 + ys[dy] * 2 + (c if core is None else core))

    other_core = device(core=oc)

    def copy(src, dst, ssem, rsem, dev):
        pltpu.make_async_remote_copy(
            src_ref=src, dst_ref=dst, send_sem=ssem, recv_sem=rsem, device_id=dev, device_id_type=MESH
        ).start()

    def wait(ref, sem):
        pltpu.make_async_copy(ref, ref, sem).wait()

    small = [(picks_in, picks), (bits_in, bits), (res_in, res)]
    small = [pltpu.make_async_copy(a, b, isem.at[i]) for i, (a, b) in enumerate(small)]

    def load(s, core):
        r = rows((s * 2 + core) * SHARD, SHARD, SHARD)
        return pltpu.make_async_copy(g.at[r], gbuf.at[r], lsem.at[s * 2 + core])

    small[0].start()
    small[1].start()
    for s in range(8):
        load(s, oc).start()
    for s in range(8):
        load(s, c).start()
    small[2].start()

    bar = pltpu.get_barrier_semaphore()

    def greet(dev):
        pl.semaphore_signal(bar, inc=1, device_id=dev, device_id_type=MESH)

    for i in FAR:
        greet(device(far=i))
    for step in NEAR:
        greet(device(*step))
    greet(other_core)

    small[0].wait()
    small[1].wait()
    for t in range(8):
        kb[t * LANES : (t + 1) * LANES, :] = spread_index(picks[t : t + 1, :])
    sgn = (1 - 2 * bits[...]).astype(F32)
    sg = [sgn[j : j + 1, :] for j in range(8)]

    def plane(core, m, start=0):
        return ((core * 8 + m) * 8) * 64 + start

    def spread(src, row0, block0):
        k = row_signs(kb[rows(block0, 8, 8), :])
        return transform([times(src[pl.ds(row0 + j, 8, stride=8), :] * sg[j], k[j]) for j in range(8)])

    def spread_shard(s, core):
        def body(i, _):
            row0 = pl.multiple_of((s * 2 + core) * SHARD + i * 64, 64)
            for m, e in enumerate(spread(gbuf, row0, (s * 2 + core) * 64 + i * 8)):
                coef[rows(plane(core, m, s * 64 + i * 8), 8, 8), :] = e
            return 0

        lax.fori_loop(0, 8, body, 0, unroll=2)

    def core_send(m):
        copy(
            coef.at[rows(plane(oc, m), 512, 512)], cin.at[m * 512 : (m + 1) * 512],
            csend.at[m], crecv.at[m], other_core,
        )

    def core_add(m):
        wait(cin.at[m * 512 : (m + 1) * 512], crecv.at[m])

        def body(i, _):
            coef[rows(plane(c, m, i * 64), 64, 64), :] += cin[rows(m * 512 + i * 64, 64, 64), :]
            return 0

        lax.fori_loop(0, 8, body, 0)

    def spread_residual():
        small[2].wait()

        def body(i, _):
            for m, e in enumerate(spread(res, pl.multiple_of(i * 64, 64), (mine * 2 + c) * 64 + i * 8)):
                rcoef[rows(m * 64 + i * 8, 8, 8), :] = e
            return 0

        lax.fori_loop(0, 8, body, 0, unroll=2)
        coef[rows(plane(c, 0, mine * 64), 64, 64), :] += rcoef[0:64, :]

    def chunk_row(dx=0, dy=0, dp=0):
        h, l = xs[dx]
        return (h * 4 + ys[dy]) * 64 + (l * 2 + zps[dp]) * CHUNK

    my_far = rows(zg * CHUNK, CHUNK, CHUNK)
    my_chunk = rows(c * 512 + chunk_row(), CHUNK, CHUNK)
    my_half = rows(c * 512, 512, 512)

    def sketch_near_send():
        for i, step in enumerate(NEAR):
            copy(
                coef.at[rows(plane(c, 0, chunk_row(*step)), CHUNK, CHUNK)],
                rsin.at[i * CHUNK : (i + 1) * CHUNK],
                rsend, rrecv, device(*step),
            )

    def sketch_far_send():
        wait(rsin, rrecv)
        total = coef[rows(plane(c, 0, chunk_row()), CHUNK, CHUNK), :]
        for i in range(31):
            total = total + rsin[i * CHUNK : (i + 1) * CHUNK, :]
        zin[my_far, :] = total
        for i in FAR:
            copy(zin.at[my_far], zin.at[my_far], zsend, zrecv, device(far=i))

    def sketch_total_send():
        wait(zin.at[0 : 7 * CHUNK], zrecv)
        z = [zin[i * CHUNK : (i + 1) * CHUNK, :] for i in range(8)]
        tot[my_chunk, :] = ((z[0] + z[1]) + (z[2] + z[3])) + ((z[4] + z[5]) + (z[6] + z[7]))
        for step in NEAR:
            copy(tot.at[my_chunk], tot.at[my_chunk], asend, arecv, device(*step))

    def sketch_half_send():
        wait(tot.at[0 : 31 * CHUNK], arecv)
        copy(tot.at[my_half], tot.at[my_half], tsend, trecv, other_core)

    def x_first_send(i):
        copy(
            coef.at[rows(plane(c, X_FIRST[i], (1 - xh) * 256), 256, 64)],
            x1in.at[i * 256 : (i + 1) * 256],
            x1s.at[i], x1r.at[i], device(dx=2),
        )

    def x_second_send(i):
        m = X_FIRST[i]
        wait(x1in.at[i * 256 : (i + 1) * 256], x1r.at[i])

        def body(k, _):
            coef[rows(plane(c, m, xh * 256 + k * 64), 64, 64), :] += x1in[rows(i * 256 + k * 64, 64, 64), :]
            return 0

        lax.fori_loop(0, 4, body, 0)
        for n, dy in enumerate((2, 1, 3)):
            copy(
                coef.at[rows(plane(c, m, (xh * 4 + ys[dy]) * 64), 64, 64)],
                y2in.at[(i * 3 + n) * 64 : (i * 3 + n + 1) * 64],
                y2s.at[i], y2r.at[i], device(dy=dy),
            )

    def y_first_send(i):
        for n, dy in enumerate((2, 1, 3)):
            for h in range(2):
                at = ((i * 3 + n) * 2 + h) * 64
                copy(
                    coef.at[rows(plane(c, Y_FIRST[i], (h * 4 + ys[dy]) * 64), 64, 64)],
                    y1in.at[at : at + 64],
                    y1s.at[i], y1r.at[i], device(dy=dy),
                )

    def y_second_send(i):
        m = Y_FIRST[i]
        wait(y1in.at[i * 384 : (i + 1) * 384], y1r.at[i])
        for h in range(2):
            a = [y1in[i * 384 + (2 * n + h) * 64 : i * 384 + (2 * n + h + 1) * 64, :] for n in range(3)]
            coef[rows(plane(c, m, (h * 4 + y) * 64), 64, 64), :] += a[0] + a[1] + a[2]
        copy(
            coef.at[rows(plane(c, m, ((1 - xh) * 4 + y) * 64), 64, 64)],
            x2in.at[i * 64 : (i + 1) * 64],
            x2s.at[i], x2r.at[i], device(dx=2),
        )

    def finish_residual():
        for i in range(len(X_FIRST)):
            wait(y2in.at[i * 192 : (i + 1) * 192], y2r.at[i])
        for i in range(len(Y_FIRST)):
            wait(x2in.at[i * 64 : (i + 1) * 64], x2r.at[i])

        def body(b, _):
            t = [None]
            for m in range(1, 8):
                e = coef[rows(plane(c, m, mine * 64 + b * 8), 8, 8), :] + rcoef[rows(m * 64 + b * 8, 8, 8), :]
                if m in X_FIRST:
                    i = X_FIRST.index(m)
                    a = [y2in[rows((i * 3 + n) * 64 + b * 8, 8, 8), :] for n in range(3)]
                    e = e + (a[0] + a[1] + a[2])
                else:
                    e = e + x2in[rows(Y_FIRST.index(m) * 64 + b * 8, 8, 8), :]
                t.append(e)
            k = row_signs(kb[rows((mine * 2 + c) * 64 + b * 8, 8, 8), :])
            for j, e in enumerate(transform(t)):
                newres[pl.ds(pl.multiple_of(b * 64, 64) + j, 8, stride=8), :] = times(e * (sg[j] * 0.125), k[j])
            return 0

        lax.fori_loop(0, 8, body, 0, unroll=2)

    for s in range(8):
        load(s, oc).wait()
        spread_shard(s, oc)
    pl.semaphore_wait(bar, 39)
    for m in range(8):
        core_send(m)
    for s in range(8):
        load(s, c).wait()
        spread_shard(s, c)
    spread_residual()
    core_add(0)
    sketch_near_send()
    for i in range(4):
        core_add(X_FIRST[i])
        x_first_send(i)
        if i < 3:
            core_add(Y_FIRST[i])
            y_first_send(i)
    sketch_far_send()
    x_second_send(0)
    y_second_send(0)
    x_second_send(1)
    y_second_send(1)
    x_second_send(2)
    y_second_send(2)
    x_second_send(3)
    sketch_total_send()
    finish_residual()
    sketch_half_send()
    wait(tot.at[my_half], trecv)

    for m in range(8):
        wait(cin.at[m * 512 : (m + 1) * 512], csend.at[m])
    wait(rsin, rsend)
    wait(zin.at[0 : 7 * CHUNK], zsend)
    wait(tot.at[0 : 31 * CHUNK], asend)
    wait(tot.at[my_half], tsend)
    for i in range(len(X_FIRST)):
        wait(x1in.at[i * 256 : (i + 1) * 256], x1s.at[i])
        wait(y2in.at[i * 192 : (i + 1) * 192], y2s.at[i])
    for i in range(len(Y_FIRST)):
        wait(y1in.at[i * 384 : (i + 1) * 384], y1s.at[i])
        wait(x2in.at[i * 64 : (i + 1) * 64], x2s.at[i])


def decode_kernel(tot, bits, picks, res_in, synced, res_out, kb, out, sem):
    res_copy = pltpu.make_async_copy(res_in, res_out, sem.at[8])
    res_copy.start()
    sgn = (1 - 2 * bits[...]).astype(F32)
    sg = [sgn[j : j + 1, :] for j in range(8)]

    def piece(s):
        at = pl.ds(s * 1024, 1024)
        return pltpu.make_async_copy(out.at[at], synced.at[at], sem.at[s])

    for s in range(8):
        kb[...] = spread_index(picks[s : s + 1, :])
        for core in range(2):

            def body(i, _, s=s, core=core):
                w = tot[rows(core * 512 + s * 64 + i * 8, 8, 8), :] * (1.0 / 256.0)
                row0 = pl.multiple_of((s * 2 + core) * SHARD + i * 64, 64)
                for j, e in enumerate(row_signs(kb[rows(core * 64 + i * 8, 8, 8), :])):
                    out[pl.ds(row0 + j, 8, stride=8), :] = times(w * sg[j], e)
                return 0

            lax.fori_loop(0, 8, body, 0, unroll=4)
        piece(s).start()
    for s in range(8):
        piece(s).wait()
    res_copy.wait()


def shards(grads, residual, sign_bits, kept_index):
    def in_hbm(a):
        return pltpu.with_memory_space_constraint(a, pltpu.HBM)

    g = in_hbm(grads.reshape(8192, LANES))
    res = in_hbm(residual.reshape(SHARD, LANES))
    bits = in_hbm(sign_bits.reshape(8, LANES))
    picks = in_hbm(kept_index.reshape(8, LANES))
    vmem = pl.BlockSpec(memory_space=pltpu.VMEM)
    hbm = pl.BlockSpec(memory_space=pltpu.HBM)
    dma = pltpu.SemaphoreType.DMA

    def buf(n, kind=F32):
        return pltpu.VMEM((n, LANES), kind)

    tot, newres = pl.pallas_call(
        comm_kernel,
        name="sum_pods",
        out_shape=(buf(1024), buf(SHARD)),
        in_specs=[hbm] * 4,
        out_specs=(vmem, vmem),
        scratch_shapes=[
            buf(512), buf(8, jnp.int32), buf(8, jnp.int32), buf(8192), buf(8192), buf(4096), buf(1024, jnp.int32), buf(512),
            buf(31 * CHUNK), buf(8 * CHUNK), buf(3 * 384), buf(4 * 256), buf(3 * 64), buf(4 * 192),
            dma((3,)), dma((16,)), dma((8,)), dma((8,)), dma, dma, dma, dma, dma, dma,
            dma, dma, dma((3,)), dma((3,)), dma((4,)), dma((4,)), dma((3,)), dma((3,)), dma((4,)), dma((4,)),
        ],
        compiler_params=pltpu.CompilerParams(
            collective_id=0, has_side_effects=True, vmem_limit_bytes=24 << 20
        ),
    )(g, res, bits, picks)

    synced, new_residual = pl.pallas_call(
        decode_kernel,
        name="decode",
        out_shape=(jax.ShapeDtypeStruct((8192, LANES), F32), jax.ShapeDtypeStruct((SHARD, LANES), F32)),
        in_specs=[vmem] * 4,
        out_specs=(hbm, hbm),
        scratch_shapes=[buf(LANES, jnp.int32), buf(8192), dma((9,))],
        compiler_params=pltpu.CompilerParams(vmem_limit_bytes=24 << 20),
    )(tot, sign_bits.reshape(8, LANES), kept_index.reshape(8, LANES), newres)
    return synced.reshape(-1), new_residual.reshape(1, -1)


def solution(mesh):
    in_specs = (P("outer", "dev", None), P("outer", "dev"), P(), P())
    out_specs = (P(), P("outer", "dev"))
    return jax.shard_map(shards, mesh=mesh, in_specs=in_specs, out_specs=out_specs, check_vma=False)
```

time: 389 us -> 49.1 us (0.13)
  waiting for transfers between devices: 253 us -> 0 us
  blocking collectives: 94.6 us -> 0 us
  Pallas kernels: 0 us -> 48.3 us
  matrix products: 15.9 us -> 0 us
  between operations: 14.8 us -> 0.67 us
  local copies, waits for them, and re-layouts: 7.42 us -> 0.01 us
    unnamed x3 -> x0, waiting for transfers between devices: 172 us -> none
    psum x1 -> x0, blocking collectives: 94.6 us -> none  [shards(): total = lax.psum(kept, 'outer')]
    all_gather x1 -> x0, waiting for transfers between devices: 81.3 us -> none  [shards(): synced = lax.all_gather(local_part, 'dev', axis=0, tiled=True)]
    pallas_call x0 -> x2, Pallas kernels: none -> 48.3 us  [the longest x1 45.7 us: shards(): pl.pallas_call(comm_kernel, name='sum_pods', out_shape=(buf(1024), buf(SH...]
    dot_general x3 -> x0, matrix products: 15.9 us -> none  [the longest x2 9.67 us: decode_runs(): jnp.dot(placed, table, precision=lax.Precision.HIGHEST) * sign_vec[None, :]]
    unnamed x10 -> x4, local copies, waits for them, and re-layouts: 6.61 us -> 0.01 us
  transfers between devices with their start and end apart: 2 -> 0, of which waited for: 2 -> 0; matrix products, arithmetic and copies ran while one was open for 2% -> 0% of each run, Pallas kernels for 0% -> 0%
where the time goes in v2:
time: 49.1 us; the launch traced here: 49 us
  Pallas kernels  48.3 us (98%)
  between operations  0.67 us (1%)
    pallas_call x1, Pallas kernels, shards(): pl.pallas_call(comm_kernel, name='sum_pods', out_shape=(buf(1024), buf(SH...  45.7 us
    pallas_call x1, Pallas kernels, shards(): pl.pallas_call(decode_kernel, name='decode', out_shape=(jax.ShapeDtypeStr...  2.6 us

profile of v2, /device:TPU:1, one launch (start us, length us, event | category | flops | bytes accessed | tf_op | source)
XLA Modules:
  0.0 49.0 jit_solution(15040553912392168360)
XLA Ops:
  0.6 0.0 copy-start.1
  0.6 0.0 copy-start
  0.7 45.7 %sum_pods.1 = (f32[1024,128]{1,0:T(8,128)S(1)}, f32[512,128]{1,0:T(8,128)S(1)}) custom-call(f32[8192,128]{1,0:T(8,128)} %bitcast.10, f32[512,128]{1,0:T(8,128)} %bitcast.11, s32[8,128]{1,0:T(8,128)} %bitcast.6, s32[8,128]{1,0:T(8,128)} %bitcast.8), custom_call_target="tpu_custom_call" | custom-call | tf_op jit(solution)/shard_map/sum_pods/pallas_call | solution.py:350
  46.3 0.0 copy-done.1
  46.3 0.0 copy-done
  46.4 2.6 %decode.1 = (f32[8192,128]{1,0:T(8,128)}, f32[512,128]{1,0:T(8,128)}) custom-call(f32[1024,128]{1,0:T(8,128)S(1)} %get-tuple-element.6.tot, s32[8,128]{1,0:T(8,128)S(1)} %bitcast.7, s32[8,128]{1,0:T(8,128)S(1)} %bitcast.9, f32[512,128]{1,0:T(8,128)S(1)} %get-tuple-element.7.res_in), custom_call_target="tpu_custom_call" | custom-call | tf_op jit(solution)/shard_map/decode/pallas_call | solution.py:367
Async XLA Ops:
  0.6 45.7 %copy-start.1 = (s32[1024]{0:T(1024)S(1)}, s32[1024]{0:T(1024)}, u32[]{:S(2)}) copy-start(s32[1024]{0:T(1024)} %param.7) | copy-start | bytes 12292
  0.6 45.7 %copy-start = (s32[1024]{0:T(1024)S(1)}, s32[1024]{0:T(1024)}, u32[]{:S(2)}) copy-start(s32[1024]{0:T(1024)} %param.6) | copy-start | bytes 12292

commit v3 on v2

--- a/solution.py
+++ b/solution.py
@@ -9,7 +9,7 @@
 F32 = jnp.float32
 LANES = 128
 SHARD = 512
-CHUNK = 16
+CHUNK = 8
 X_FIRST = (1, 3, 5, 7)
 Y_FIRST = (2, 4, 6)
 NEAR = sorted(
@@ -51,7 +51,7 @@
 def comm_kernel(
     g, res_in, bits_in, picks_in, tot, newres,
     res, bits, picks, gbuf, coef, cin, kb, rcoef, rsin, zin, y1in, x1in, x2in, y2in,
-    isem, lsem, csend, crecv, rsend, rrecv, zsend, zrecv, asend, arecv,
+    isem, lsem, relay1, relay2, upper, ksend, krecv, csend, crecv, rsend, rrecv, zsend, zrecv, asend, arecv,
     tsend, trecv, y1s, y1r, x1s, x1r, x2s, x2r, y2s, y2r,
 ):
     o, d = lax.axis_index("outer"), lax.axis_index("dev")
@@ -88,22 +88,59 @@
 
     small[0].start()
     small[1].start()
-    for s in range(8):
+    for s in range(4):
         load(s, oc).start()
-    for s in range(8):
+    small[2].start()
+    for s in range(4):
         load(s, c).start()
-    small[2].start()
+    for s in range(4, 8):
+        load(s, oc).start()
+    for s in range(4, 8):
+        load(s, c).start()
 
     bar = pltpu.get_barrier_semaphore()
 
-    def greet(dev):
-        pl.semaphore_signal(bar, inc=1, device_id=dev, device_id_type=MESH)
-
-    for i in FAR:
-        greet(device(far=i))
+    def signal(sem, dev):
+        pl.semaphore_signal(sem, inc=1, device_id=dev, device_id_type=MESH)
+
     for step in NEAR:
-        greet(device(*step))
-    greet(other_core)
+        signal(bar, device(*step))
+    signal(bar, other_core)
+
+    upper_half, zq = zg // 4, zg % 4
+
+    def layer(t):
+        return (xl * 16 + t * 2 + zp, xh * 8 + y * 2 + c)
+
+    def neighbours(below, above):
+        pl.when(zq > 0)(below)
+        pl.when(zq < 3)(above)
+
+    neighbours(lambda: signal(bar, layer(zg - 1)), lambda: signal(bar, layer(zg + 1)))
+
+    @pl.when(upper_half == 0)
+    def _():
+        for t in range(4, 8):
+            signal(bar, layer(t))
+
+    def enter():
+        pl.semaphore_wait(bar, 32 + (zq + 3) // 4 + (6 - zq) // 4 + 4 * upper_half)
+        neighbours(lambda: signal(relay1.at[1], layer(zg - 1)), lambda: signal(relay1.at[0], layer(zg + 1)))
+
+        @pl.when(upper_half == 1)
+        def _():
+            for t in range(4):
+                signal(upper, layer(t))
+
+    def pass_on():
+        neighbours(lambda: pl.semaphore_wait(relay1.at[0], 1), lambda: pl.semaphore_wait(relay1.at[1], 1))
+        pl.when(zq == 1)(lambda: signal(relay2, layer(zg + 2)))
+        pl.when(zq == 2)(lambda: signal(relay2, layer(zg - 2)))
+
+    def hear_all():
+        pl.when(zq == 0)(lambda: pl.semaphore_wait(relay2, 1))
+        pl.when(zq == 3)(lambda: pl.semaphore_wait(relay2, 1))
+        pl.when(upper_half == 0)(lambda: pl.semaphore_wait(upper, 4))
 
     small[0].wait()
     small[1].wait()
@@ -115,6 +152,23 @@
     def plane(core, m, start=0):
         return ((core * 8 + m) * 8) * 64 + start
 
+    def fold_shard(s, core):
+        def body(i, _):
+            row0 = pl.multiple_of((s * 2 + core) * SHARD + i * 64, 64)
+            e = fold(gbuf, row0, (s * 2 + core) * 64 + i * 8)
+            coef[rows(plane(core, 0, s * 64 + i * 8), 8, 8), :] = e
+            return 0
+
+        lax.fori_loop(0, 8, body, 0, unroll=4)
+
+    def fold(src, row0, block0):
+        k = kb[rows(block0, 8, 8), :]
+        t = [src[pl.ds(row0 + j, 8, stride=8), :] * sg[j] for j in range(8)]
+        for bit in range(3):
+            sign = (1 - 2 * ((k >> bit) & 1)).astype(F32)
+            t = [t[i] + sign * t[i + 1] for i in range(0, len(t), 2)]
+        return t[0]
+
     def spread(src, row0, block0):
         k = row_signs(kb[rows(block0, 8, 8), :])
         return transform([times(src[pl.ds(row0 + j, 8, stride=8), :] * sg[j], k[j]) for j in range(8)])
@@ -122,7 +176,7 @@
     def spread_shard(s, core):
         def body(i, _):
             row0 = pl.multiple_of((s * 2 + core) * SHARD + i * 64, 64)
-            for m, e in enumerate(spread(gbuf, row0, (s * 2 + core) * 64 + i * 8)):
+            for m, e in enumerate(spread(gbuf, row0, (s * 2 + core) * 64 + i * 8)[1:], 1):
                 coef[rows(plane(core, m, s * 64 + i * 8), 8, 8), :] = e
             return 0
 
@@ -144,51 +198,67 @@
         lax.fori_loop(0, 8, body, 0)
 
     def spread_residual():
-        small[2].wait()
-
         def body(i, _):
             for m, e in enumerate(spread(res, pl.multiple_of(i * 64, 64), (mine * 2 + c) * 64 + i * 8)):
                 rcoef[rows(m * 64 + i * 8, 8, 8), :] = e
             return 0
 
         lax.fori_loop(0, 8, body, 0, unroll=2)
-        coef[rows(plane(c, 0, mine * 64), 64, 64), :] += rcoef[0:64, :]
 
     def chunk_row(dx=0, dy=0, dp=0):
         h, l = xs[dx]
-        return (h * 4 + ys[dy]) * 64 + (l * 2 + zps[dp]) * CHUNK
-
-    my_far = rows(zg * CHUNK, CHUNK, CHUNK)
-    my_chunk = rows(c * 512 + chunk_row(), CHUNK, CHUNK)
-    my_half = rows(c * 512, 512, 512)
-
-    def sketch_near_send():
+        return ((h * 4 + ys[dy]) * 4 + l * 2 + zps[dp]) * CHUNK
+
+    def half(q):
+        return pl.ds(q * 256, 256)
+
+    def far_rows(q):
+        return rows((q * 8 + zg) * CHUNK, CHUNK, CHUNK)
+
+    def total_chunk(q):
+        return rows(c * 512 + q * 256 + chunk_row(), CHUNK, CHUNK)
+
+    def total_half(q):
+        return rows(c * 512 + q * 256, 256, 256)
+
+    def sketch_core_send(q):
+        copy(coef.at[rows(plane(oc, 0, q * 256), 256, 256)], cin.at[half(q)], ksend.at[q], krecv.at[q], other_core)
+
+    def sketch_core_add(q):
+        wait(cin.at[half(q)], krecv.at[q])
+        for s in range(4 * q, 4 * q + 4):
+            at = rows(plane(c, 0, s * 64), 64, 64)
+            own = jnp.where(mine == s, 1.0, 0.0).astype(F32)
+            coef[at, :] += cin[s * 64 : (s + 1) * 64, :] + own * rcoef[0:64, :]
+
+    def sketch_near_send(q):
         for i, step in enumerate(NEAR):
+            at = (q * 31 + i) * CHUNK
             copy(
-                coef.at[rows(plane(c, 0, chunk_row(*step)), CHUNK, CHUNK)],
-                rsin.at[i * CHUNK : (i + 1) * CHUNK],
-                rsend, rrecv, device(*step),
+                coef.at[rows(plane(c, 0, q * 256 + chunk_row(*step)), CHUNK, CHUNK)],
+                rsin.at[at : at + CHUNK],
+                rsend.at[q], rrecv.at[q], device(*step),
             )
 
-    def sketch_far_send():
-        wait(rsin, rrecv)
-        total = coef[rows(plane(c, 0, chunk_row()), CHUNK, CHUNK), :]
+    def sketch_far_send(q):
+        wait(rsin.at[q * 31 * CHUNK : (q + 1) * 31 * CHUNK], rrecv.at[q])
+        total = coef[rows(plane(c, 0, q * 256 + chunk_row()), CHUNK, CHUNK), :]
         for i in range(31):
-            total = total + rsin[i * CHUNK : (i + 1) * CHUNK, :]
-        zin[my_far, :] = total
+            total = total + rsin[(q * 31 + i) * CHUNK : (q * 31 + i + 1) * CHUNK, :]
+        zin[far_rows(q), :] = total
         for i in FAR:
-            copy(zin.at[my_far], zin.at[my_far], zsend, zrecv, device(far=i))
-
-    def sketch_total_send():
-        wait(zin.at[0 : 7 * CHUNK], zrecv)
-        z = [zin[i * CHUNK : (i + 1) * CHUNK, :] for i in range(8)]
-        tot[my_chunk, :] = ((z[0] + z[1]) + (z[2] + z[3])) + ((z[4] + z[5]) + (z[6] + z[7]))
+            copy(zin.at[far_rows(q)], zin.at[far_rows(q)], zsend.at[q], zrecv.at[q], device(far=i))
+
+    def sketch_total_send(q):
+        wait(zin.at[q * 8 * CHUNK : (q * 8 + 7) * CHUNK], zrecv.at[q])
+        z = [zin[(q * 8 + i) * CHUNK : (q * 8 + i + 1) * CHUNK, :] for i in range(8)]
+        tot[total_chunk(q), :] = ((z[0] + z[1]) + (z[2] + z[3])) + ((z[4] + z[5]) + (z[6] + z[7]))
         for step in NEAR:
-            copy(tot.at[my_chunk], tot.at[my_chunk], asend, arecv, device(*step))
-
-    def sketch_half_send():
-        wait(tot.at[0 : 31 * CHUNK], arecv)
-        copy(tot.at[my_half], tot.at[my_half], tsend, trecv, other_core)
+            copy(tot.at[total_chunk(q)], tot.at[total_chunk(q)], asend.at[q], arecv.at[q], device(*step))
+
+    def sketch_half_send(q):
+        wait(tot.at[0 : 31 * CHUNK], arecv.at[q])
+        copy(tot.at[total_half(q)], tot.at[total_half(q)], tsend.at[q], trecv.at[q], other_core)
 
     def x_first_send(i):
         copy(
@@ -259,43 +329,57 @@
 
         lax.fori_loop(0, 8, body, 0, unroll=2)
 
+    for q in range(2):
+        for s in range(4 * q, 4 * q + 4):
+            load(s, oc).wait()
+            fold_shard(s, oc)
+        if q == 0:
+            enter()
+        sketch_core_send(q)
+        for s in range(4 * q, 4 * q + 4):
+            load(s, c).wait()
+            fold_shard(s, c)
+        if q == 0:
+            small[2].wait()
+            spread_residual()
+        sketch_core_add(q)
+        sketch_near_send(q)
+    pass_on()
     for s in range(8):
-        load(s, oc).wait()
         spread_shard(s, oc)
-    pl.semaphore_wait(bar, 39)
-    for m in range(8):
+    for m in range(1, 8):
         core_send(m)
     for s in range(8):
-        load(s, c).wait()
         spread_shard(s, c)
-    spread_residual()
-    core_add(0)
-    sketch_near_send()
     for i in range(4):
         core_add(X_FIRST[i])
         x_first_send(i)
         if i < 3:
             core_add(Y_FIRST[i])
             y_first_send(i)
-    sketch_far_send()
-    x_second_send(0)
-    y_second_send(0)
-    x_second_send(1)
-    y_second_send(1)
-    x_second_send(2)
-    y_second_send(2)
-    x_second_send(3)
-    sketch_total_send()
+    hear_all()
+    sketch_far_send(0)
+    sketch_far_send(1)
+    for i in range(4):
+        x_second_send(i)
+        if i < 3:
+            y_second_send(i)
+    sketch_total_send(0)
+    sketch_total_send(1)
     finish_residual()
-    sketch_half_send()
-    wait(tot.at[my_half], trecv)
-
-    for m in range(8):
+    sketch_half_send(0)
+    sketch_half_send(1)
+    wait(tot.at[total_half(0)], trecv.at[0])
+    wait(tot.at[total_half(1)], trecv.at[1])
+
+    for q in range(2):
+        wait(cin.at[half(q)], ksend.at[q])
+        wait(rsin.at[q * 31 * CHUNK : (q + 1) * 31 * CHUNK], rsend.at[q])
+        wait(zin.at[0 : 7 * CHUNK], zsend.at[q])
+        wait(tot.at[0 : 31 * CHUNK], asend.at[q])
+        wait(tot.at[total_half(q)], tsend.at[q])
+    for m in range(1, 8):
         wait(cin.at[m * 512 : (m + 1) * 512], csend.at[m])
-    wait(rsin, rsend)
-    wait(zin.at[0 : 7 * CHUNK], zsend)
-    wait(tot.at[0 : 31 * CHUNK], asend)
-    wait(tot.at[my_half], tsend)
     for i in range(len(X_FIRST)):
         wait(x1in.at[i * 256 : (i + 1) * 256], x1s.at[i])
         wait(y2in.at[i * 192 : (i + 1) * 192], y2s.at[i])
@@ -355,9 +439,10 @@
         out_specs=(vmem, vmem),
         scratch_shapes=[
             buf(512), buf(8, jnp.int32), buf(8, jnp.int32), buf(8192), buf(8192), buf(4096), buf(1024, jnp.int32), buf(512),
-            buf(31 * CHUNK), buf(8 * CHUNK), buf(3 * 384), buf(4 * 256), buf(3 * 64), buf(4 * 192),
-            dma((3,)), dma((16,)), dma((8,)), dma((8,)), dma, dma, dma, dma, dma, dma,
-            dma, dma, dma((3,)), dma((3,)), dma((4,)), dma((4,)), dma((3,)), dma((3,)), dma((4,)), dma((4,)),
+            buf(62 * CHUNK), buf(16 * CHUNK), buf(3 * 384), buf(4 * 256), buf(3 * 64), buf(4 * 192),
+            dma((3,)), dma((16,)), pltpu.SemaphoreType.REGULAR((2,)), pltpu.SemaphoreType.REGULAR, pltpu.SemaphoreType.REGULAR,
+            dma((2,)), dma((2,)), dma((8,)), dma((8,)), dma((2,)), dma((2,)), dma((2,)), dma((2,)), dma((2,)), dma((2,)),
+            dma((2,)), dma((2,)), dma((3,)), dma((3,)), dma((4,)), dma((4,)), dma((3,)), dma((3,)), dma((4,)), dma((4,)),
         ],
         compiler_params=pltpu.CompilerParams(
             collective_id=0, has_side_effects=True, vmem_limit_bytes=24 << 20

time: 49.1 us -> 42.1 us (0.86)
  Pallas kernels: 48.3 us -> 41.3 us
    pallas_call x1, Pallas kernels: 45.7 us -> 38.7 us  [shards(): pl.pallas_call(comm_kernel, name='sum_pods', out_shape=(buf(1024), buf(SH...]
where the time goes in v3:
time: 42.1 us; the launch traced here: 42 us
  Pallas kernels  41.3 us (98%)
  between operations  0.67 us (2%)
    pallas_call x1, Pallas kernels, shards(): pl.pallas_call(comm_kernel, name='sum_pods', out_shape=(buf(1024), buf(SH...  38.7 us
    pallas_call x1, Pallas kernels, shards(): pl.pallas_call(decode_kernel, name='decode', out_shape=(jax.ShapeDtypeStr...  2.6 us

profile of v3, /device:TPU:1, one launch (start us, length us, event | category | flops | bytes accessed | tf_op | source)
XLA Modules:
  0.0 42.0 jit_solution(9936252275122523501)
XLA Ops:
  0.6 0.0 copy-start.1
  0.6 0.0 copy-start
  0.7 38.7 %sum_pods.1 = (f32[1024,128]{1,0:T(8,128)S(1)}, f32[512,128]{1,0:T(8,128)S(1)}) custom-call(f32[8192,128]{1,0:T(8,128)} %bitcast.10, f32[512,128]{1,0:T(8,128)} %bitcast.11, s32[8,128]{1,0:T(8,128)} %bitcast.6, s32[8,128]{1,0:T(8,128)} %bitcast.8), custom_call_target="tpu_custom_call" | custom-call | tf_op jit(solution)/shard_map/sum_pods/pallas_call | solution.py:434
  39.3 0.0 copy-done.1
  39.3 0.0 copy-done
  39.4 2.6 %decode.1 = (f32[8192,128]{1,0:T(8,128)}, f32[512,128]{1,0:T(8,128)}) custom-call(f32[1024,128]{1,0:T(8,128)S(1)} %get-tuple-element.6.tot, s32[8,128]{1,0:T(8,128)S(1)} %bitcast.7, s32[8,128]{1,0:T(8,128)S(1)} %bitcast.9, f32[512,128]{1,0:T(8,128)S(1)} %get-tuple-element.7.res_in), custom_call_target="tpu_custom_call" | custom-call | tf_op jit(solution)/shard_map/decode/pallas_call | solution.py:452
Async XLA Ops:
  0.6 38.7 %copy-start.1 = (s32[1024]{0:T(1024)S(1)}, s32[1024]{0:T(1024)}, u32[]{:S(2)}) copy-start(s32[1024]{0:T(1024)} %param.7) | copy-start | bytes 12292
  0.6 38.7 %copy-start = (s32[1024]{0:T(1024)S(1)}, s32[1024]{0:T(1024)}, u32[]{:S(2)}) copy-start(s32[1024]{0:T(1024)} %param.6) | copy-start | bytes 12292
